TPU v7x, 32 devices: a whole 2x2x4 slice. The times are simulated.
32 devices in a mesh: ctx: 8 (over y, x, core), tp: 4 (over z).
Axes of the slice: x: 2, y: 2, z: 4, core: 2. Of those that a mesh axis runs over, the one named last changes fastest.
Arguments:
- queries: bfloat16 [2048, 8192], P('ctx', 'tp'), may hold values from -120 to 120
- key_proj: bfloat16 [2048, 1024], P('ctx', 'tp'), may hold values from -4 to 4
- value_proj: bfloat16 [2048, 1024], P('ctx', 'tp'), may hold values from -6 to 6
- out_weight: bfloat16 [8192, 8192], P('tp'), may hold values from -0.75 to 0.75
- doc_ids: int32 [2048], replicated, may hold values from 0 to 7, never falling along the last dimension, each value on 1 to 1024 neighbouring positions
- drop_seed: int32 [1], replicated, may hold values from 0 to 1073741823
Outputs:
- output: bfloat16 [2048, 8192], P('ctx', 'tp')
Inputs may be any that keep to these rules, and one draw needn't show every extreme that they name: doc_ids never fall along the sequence; each document has 1 to 1024 tokens, one exactly 1024.
All inputs are finite; a program needn't handle non-finite values.
Results may differ from a plain program's by a relative error of at most 0.019.
Values may be sent and summed in bfloat16 or wider, within the bound.
A program may use at most 128 MiB of HBM per device.

v0:
```python
import math

import jax
import jax.numpy as jnp
from jax import lax
from jax.sharding import PartitionSpec as P

HEADS = 64
KVH = 8
HD = 128


def mixing(value):
    value = value ^ lax.shift_right_logical(value, jnp.int32(16))
    value = value * 73244475
    value = value ^ lax.shift_right_logical(value, jnp.int32(16))
    value = value * 73244475
    value = value ^ lax.shift_right_logical(value, jnp.int32(16))
    return value


def attend_tile(state, context, k_block, v_block, k_start):
    q_heads, q_pos, q_doc, q_hash, doc_ids = context
    count = k_block.shape[0]
    local_kv = q_heads.shape[1]
    k_pos = k_start + jnp.arange(count, dtype=jnp.int32)
    k_doc = lax.dynamic_slice_in_dim(doc_ids, k_start, count)
    peak, row_sum, accum = state
    k_heads = k_block.reshape(count, local_kv, HD)
    v_heads = v_block.reshape(count, local_kv, HD)
    scores = jnp.einsum(
        "qkgd,nkd->qkgn", q_heads, k_heads, preferred_element_type=jnp.float32
    ) * HD ** (-0.5)
    allowed = (q_doc[:, None] == k_doc[None, :]) & (k_pos[None, :] <= q_pos[:, None])
    allowed = allowed[:, None, None, :]
    row_max = jnp.max(jnp.where(allowed, scores, jnp.float32(-1e30)), axis=-1)
    new_peak = jnp.maximum(peak, row_max)
    rescale = jnp.exp(peak - new_peak)
    weights = jnp.where(allowed, jnp.exp(scores - new_peak[..., None]), jnp.float32(0.0))
    row_sum = row_sum * rescale + jnp.sum(weights, axis=-1)
    full_hash = mixing(q_hash + k_pos.reshape(1, 1, 1, count))
    keeper = lax.shift_right_logical(full_hash, jnp.int32(8)) >= 1677722
    dropped = jnp.where(keeper, weights * jnp.float32(1.0 / 0.9), jnp.float32(0.0)).astype(
        jnp.bfloat16
    )
    accum = accum * rescale[..., None] + jnp.einsum(
        "qkgn,nkd->qkgd", dropped, v_heads, preferred_element_type=jnp.float32
    )
    return (new_peak, row_sum, accum)


def attend_range(state, context, k_rows, v_rows):
    count = k_rows.shape[0]
    tile_rows = math.gcd(count, 512)

    def step_tile(number, current):
        offset = number * tile_rows
        k_tile = lax.dynamic_slice_in_dim(k_rows, offset, tile_rows, 0)
        v_tile = lax.dynamic_slice_in_dim(v_rows, offset, tile_rows, 0)
        return attend_tile(current, context, k_tile, v_tile, offset)

    return lax.fori_loop(0, count // tile_rows, step_tile, state)


def body(queries, key_proj, value_proj, out_weight, doc_ids, drop_seed):
    tok_rows = queries.shape[0]
    half_rows = tok_rows // 2
    local_kv = key_proj.shape[1] // HD
    per_group = HEADS // KVH
    ctx_index = lax.axis_index("ctx")
    tp_index = lax.axis_index("tp")
    head_ids = tp_index * (local_kv * per_group) + jnp.arange(local_kv * per_group, dtype=jnp.int32)
    head_ids = head_ids.reshape(1, local_kv, per_group, 1)
    seed_value = drop_seed[0]
    half_index = jnp.arange(half_rows, dtype=jnp.int32)
    first_q = queries[:half_rows]
    second_q = queries[half_rows:]
    first_pos = ctx_index * tok_rows + half_index
    second_pos = ctx_index * tok_rows + half_rows + half_index
    contexts = []
    for half_q, half_pos in ((first_q, first_pos), (second_q, second_pos)):
        q_heads = half_q.reshape(half_rows, local_kv, per_group, HD)
        q_doc = lax.dynamic_slice_in_dim(doc_ids, half_pos[0], half_rows)
        q_hash = mixing(
            mixing(seed_value * 7919 + head_ids) ^ half_pos.reshape(half_rows, 1, 1, 1) * 65537
        )
        contexts.append((q_heads, half_pos, q_doc, q_hash, doc_ids))

    def start_state():
        return (
            jnp.full((half_rows, local_kv, per_group), -1e30, jnp.float32),
            jnp.zeros((half_rows, local_kv, per_group), jnp.float32),
            jnp.zeros((half_rows, local_kv, per_group, HD), jnp.float32),
        )

    piece = (
        lax.all_gather(key_proj, "ctx", axis=0, tiled=True),
        lax.all_gather(value_proj, "ctx", axis=0, tiled=True),
    )
    final = (
        attend_range(start_state(), contexts[0], piece[0], piece[1]),
        attend_range(start_state(), contexts[1], piece[0], piece[1]),
    )
    halves = []
    for state in final:
        peak, row_sum, accum = state
        halves.append(
            (accum / row_sum[..., None])
            .astype(jnp.bfloat16)
            .reshape(half_rows, local_kv * per_group * HD)
        )
    second_rows = halves[1]
    attention = jnp.concatenate([halves[0], second_rows], axis=0)
    partial_value = jnp.dot(attention, out_weight, preferred_element_type=jnp.float32)
    return lax.psum_scatter(
        partial_value.astype(jnp.bfloat16), "tp", scatter_dimension=1, tiled=True
    )


def solution(mesh):
    in_specs = (P("ctx", "tp"), P("ctx", "tp"), P("ctx", "tp"), P("tp", None), P(), P())
    out_specs = P("ctx", "tp")
    return jax.shard_map(body, mesh=mesh, in_specs=in_specs, out_specs=out_specs, check_vma=False)
```

profile of v0, /device:TPU:15, one launch (start us, length us, event | category | flops | bytes accessed | tf_op | source)
XLA Modules:
  0.0 247.8 jit_solution(9483271076004990414)
XLA Ops:
  13.6 19.9 %all-gather.3.cloned.1.call-done = bf16[2048,256]{0,1:T(8,128)(2,1)} async-done(((bf16[256,256]{0,1:T(8,128)(2,1)}), bf16[2048,256]{0,1:T(8,128)(2,1)}) %all-gather.3.cloned.1.call-update) | async-done | bytes 1048592 | tf_op jit(solution)/shard_map/all_gather | solution.py:97
  33.4 25.5 %all-gather.5.cloned.1.call-done = bf16[2048,256]{0,1:T(8,128)(2,1)} async-done(((bf16[256,256]{0,1:T(8,128)(2,1)}), bf16[2048,256]{0,1:T(8,128)(2,1)}) %all-gather.5.cloned.1.call-update) | async-done | bytes 1048592 | tf_op jit(solution)/shard_map/all_gather | solution.py:98
  58.9 45.9 %while.36 = (s32[]{:T(128)}, f32[128,2,8]{0,2,1:T(8,128)S(1)}, f32[128,2,8]{0,2,1:T(8,128)S(1)}, f32[128,2,8,128]{0,3,2,1:T(8,128)}, s32[128]{0:T(128)S(1)}, /*i...) while((s32[]{:T(128)}, f32[128,2,8]{0,2,1:T(8,128)S(1)}, ...), condition=%wide.region_3.4_spmd.clone, body=%wide.region_0.3_spmd.clone.sunk | while | flops 563049088 | bytes 42367344 | solution.py:62
  63.1 3.2 %fusion.87 = f32[128,2,8]{0,2,1:T(8,128)S(1)} fusion(f32[2,512,128,8]{2,1,3,0:T(8,128)} %get-tuple-element.708, f32[128,2,8]{0,2,1:T(8,128)S(1)} %select_maximum_fusion.4, pred[128,512]{0,1:T(8,128)(4,1)S(1)} %compare_and_fusion.4), kind=kLoop, calls=%fused_computation.17.clone.1 | loop fusion | flops 4192256 | bytes 4276224 | tf_op jit(solution)/shard_map/while/body/eval_jaxpr/reduce_sum | solution.py:40
  66.5 2.9 %fusion.90 = f32[128,2,8,128]{0,3,2,1:T(8,128)S(1)} fusion(bf16[512,2,128,1]{0,2,3,1:T(8,128)(2,1)S(1)} %bitcast.126, f32[2,512,128,8]{2,1,3,0:T(8,128)S(1)} %copy-done, s32[512]{0:T(512)S(1)} %iota_add_fusion.11, s32[128,2,8]{0,2,1:T(8,128)S(1)} %fusion.89, f32[128,2,8]{0,2,1:T(8,128)S(1)} %select_maximum_fusion.4, ...), kind=kOutput, calls=%fused_computation.20.clone.1 | convolution fusion | flops 287047680 | bytes 6645761 | tf_op jit(solution)/shard_map/while/body/eval_jaxpr/qkgn,nkd->qkgd/dot_general | solution.py:46
  74.6 3.2 %fusion.87 = f32[128,2,8]{0,2,1:T(8,128)S(1)} fusion(f32[2,512,128,8]{2,1,3,0:T(8,128)} %get-tuple-element.708, f32[128,2,8]{0,2,1:T(8,128)S(1)} %select_maximum_fusion.4, pred[128,512]{0,1:T(8,128)(4,1)S(1)} %compare_and_fusion.4), kind=kLoop, calls=%fused_computation.17.clone.1 | loop fusion | flops 4192256 | bytes 4276224 | tf_op jit(solution)/shard_map/while/body/eval_jaxpr/reduce_sum | solution.py:40
  78.0 2.9 %fusion.90 = f32[128,2,8,128]{0,3,2,1:T(8,128)S(1)} fusion(bf16[512,2,128,1]{0,2,3,1:T(8,128)(2,1)S(1)} %bitcast.126, f32[2,512,128,8]{2,1,3,0:T(8,128)S(1)} %copy-done, s32[512]{0:T(512)S(1)} %iota_add_fusion.11, s32[128,2,8]{0,2,1:T(8,128)S(1)} %fusion.89, f32[128,2,8]{0,2,1:T(8,128)S(1)} %select_maximum_fusion.4, ...), kind=kOutput, calls=%fused_computation.20.clone.1 | convolution fusion | flops 287047680 | bytes 6645761 | tf_op jit(solution)/shard_map/while/body/eval_jaxpr/qkgn,nkd->qkgd/dot_general | solution.py:46
  83.2 2.8 %fusion.86 = (f32[128,2,8]{0,2,1:T(8,128)S(1)}, f32[2,512,128,8]{2,1,3,0:T(8,128)}) fusion(pred[128,512]{0,1:T(8,128)(4,1)S(1)} %compare_and_fusion.4, bf16[512,2,128,1]{0,2,3,1:T(8,128)(2,1)S(1)} %bitcast.124, bf16[128,2,8,128]{3,0,2,1:T(8,128)(2,1)S(1)} %get-tuple-element.817), kind=kOutput, calls=%fused_computation.13.clone.1 | convolution fusion | flops 271579136 | bytes 5054464 | tf_op jit(solution)/shard_map/while/body/eval_jaxpr/qkgd,nkd->qkgn/dot_general | solution.py:31
  86.0 3.2 %fusion.87 = f32[128,2,8]{0,2,1:T(8,128)S(1)} fusion(f32[2,512,128,8]{2,1,3,0:T(8,128)} %get-tuple-element.708, f32[128,2,8]{0,2,1:T(8,128)S(1)} %select_maximum_fusion.4, pred[128,512]{0,1:T(8,128)(4,1)S(1)} %compare_and_fusion.4), kind=kLoop, calls=%fused_computation.17.clone.1 | loop fusion | flops 4192256 | bytes 4276224 | tf_op jit(solution)/shard_map/while/body/eval_jaxpr/reduce_sum | solution.py:40
  89.5 2.9 %fusion.90 = f32[128,2,8,128]{0,3,2,1:T(8,128)S(1)} fusion(bf16[512,2,128,1]{0,2,3,1:T(8,128)(2,1)S(1)} %bitcast.126, f32[2,512,128,8]{2,1,3,0:T(8,128)S(1)} %copy-done, s32[512]{0:T(512)S(1)} %iota_add_fusion.11, s32[128,2,8]{0,2,1:T(8,128)S(1)} %fusion.89, f32[128,2,8]{0,2,1:T(8,128)S(1)} %select_maximum_fusion.4, ...), kind=kOutput, calls=%fused_computation.20.clone.1 | convolution fusion | flops 287047680 | bytes 6645761 | tf_op jit(solution)/shard_map/while/body/eval_jaxpr/qkgn,nkd->qkgd/dot_general | solution.py:46
  97.5 3.2 %fusion.87 = f32[128,2,8]{0,2,1:T(8,128)S(1)} fusion(f32[2,512,128,8]{2,1,3,0:T(8,128)} %get-tuple-element.708, f32[128,2,8]{0,2,1:T(8,128)S(1)} %select_maximum_fusion.4, pred[128,512]{0,1:T(8,128)(4,1)S(1)} %compare_and_fusion.4), kind=kLoop, calls=%fused_computation.17.clone.1 | loop fusion | flops 4192256 | bytes 4276224 | tf_op jit(solution)/shard_map/while/body/eval_jaxpr/reduce_sum | solution.py:40
  100.9 2.9 %fusion.90 = f32[128,2,8,128]{0,3,2,1:T(8,128)S(1)} fusion(bf16[512,2,128,1]{0,2,3,1:T(8,128)(2,1)S(1)} %bitcast.126, f32[2,512,128,8]{2,1,3,0:T(8,128)S(1)} %copy-done, s32[512]{0:T(512)S(1)} %iota_add_fusion.11, s32[128,2,8]{0,2,1:T(8,128)S(1)} %fusion.89, f32[128,2,8]{0,2,1:T(8,128)S(1)} %select_maximum_fusion.4, ...), kind=kOutput, calls=%fused_computation.20.clone.1 | convolution fusion | flops 287047680 | bytes 6645761 | tf_op jit(solution)/shard_map/while/body/eval_jaxpr/qkgn,nkd->qkgd/dot_general | solution.py:46
  104.8 42.1 %while.37 = (s32[]{:T(128)}, f32[128,2,8]{0,2,1:T(8,128)S(1)}, f32[128,2,8]{0,2,1:T(8,128)S(1)}, f32[128,2,8,128]{0,3,2,1:T(8,128)S(1)}, s32[128]{0:T(128)S(1)},...) while((s32[]{:T(128)}, f32[128,2,8]{0,2,1:T(8,128)S(1)}, ...), condition=%wide.region_7.8_spmd.clone, body=%wide.region_4.7_spmd.clone.sunk | while | flops 563049088 | bytes 33978680 | solution.py:62
  106.2 2.8 %fusion.94 = (f32[128,2,8]{0,2,1:T(8,128)S(1)}, f32[2,512,128,8]{2,1,3,0:T(8,128)}) fusion(pred[128,512]{0,1:T(8,128)(4,1)S(1)} %compare_and_fusion.5, bf16[512,2,128,1]{0,2,3,1:T(8,128)(2,1)S(1)} %bitcast.125, bf16[128,2,8,128]{3,0,2,1:T(8,128)(2,1)S(1)} %get-tuple-element.769), kind=kOutput, calls=%fused_computation.53.clone.1 | convolution fusion | flops 271579136 | bytes 5054464 | tf_op jit(solution)/shard_map/while/body/eval_jaxpr/qkgd,nkd->qkgn/dot_general | solution.py:31
  109.0 3.2 %fusion.95 = f32[128,2,8]{0,2,1:T(8,128)S(1)} fusion(f32[2,512,128,8]{2,1,3,0:T(8,128)} %get-tuple-element.726, f32[128,2,8]{0,2,1:T(8,128)S(1)} %select_maximum_fusion.5, pred[128,512]{0,1:T(8,128)(4,1)S(1)} %compare_and_fusion.5), kind=kLoop, calls=%fused_computation.57.clone.1 | loop fusion | flops 4192256 | bytes 4276224 | tf_op jit(solution)/shard_map/while/body/eval_jaxpr/reduce_sum | solution.py:40
  112.4 2.9 %fusion.98 = f32[128,2,8,128]{0,3,2,1:T(8,128)S(1)} fusion(bf16[512,2,128,1]{0,2,3,1:T(8,128)(2,1)S(1)} %bitcast.127, f32[2,512,128,8]{2,1,3,0:T(8,128)S(1)} %copy-done.1, s32[512]{0:T(512)S(1)} %iota_add_fusion.13, s32[128,2,8]{0,2,1:T(8,128)S(1)} %fusion.97, f32[128,2,8]{0,2,1:T(8,128)S(1)} %select_maximum_fusion.5, ...), kind=kOutput, calls=%fused_computation.60.clone.1 | convolution fusion | flops 287047680 | bytes 6645761 | tf_op jit(solution)/shard_map/while/body/eval_jaxpr/qkgn,nkd->qkgd/dot_general | solution.py:46
  119.5 3.2 %fusion.95 = f32[128,2,8]{0,2,1:T(8,128)S(1)} fusion(f32[2,512,128,8]{2,1,3,0:T(8,128)} %get-tuple-element.726, f32[128,2,8]{0,2,1:T(8,128)S(1)} %select_maximum_fusion.5, pred[128,512]{0,1:T(8,128)(4,1)S(1)} %compare_and_fusion.5), kind=kLoop, calls=%fused_computation.57.clone.1 | loop fusion | flops 4192256 | bytes 4276224 | tf_op jit(solution)/shard_map/while/body/eval_jaxpr/reduce_sum | solution.py:40
  122.9 2.9 %fusion.98 = f32[128,2,8,128]{0,3,2,1:T(8,128)S(1)} fusion(bf16[512,2,128,1]{0,2,3,1:T(8,128)(2,1)S(1)} %bitcast.127, f32[2,512,128,8]{2,1,3,0:T(8,128)S(1)} %copy-done.1, s32[512]{0:T(512)S(1)} %iota_add_fusion.13, s32[128,2,8]{0,2,1:T(8,128)S(1)} %fusion.97, f32[128,2,8]{0,2,1:T(8,128)S(1)} %select_maximum_fusion.5, ...), kind=kOutput, calls=%fused_computation.60.clone.1 | convolution fusion | flops 287047680 | bytes 6645761 | tf_op jit(solution)/shard_map/while/body/eval_jaxpr/qkgn,nkd->qkgd/dot_general | solution.py:46
  130.0 3.2 %fusion.95 = f32[128,2,8]{0,2,1:T(8,128)S(1)} fusion(f32[2,512,128,8]{2,1,3,0:T(8,128)} %get-tuple-element.726, f32[128,2,8]{0,2,1:T(8,128)S(1)} %select_maximum_fusion.5, pred[128,512]{0,1:T(8,128)(4,1)S(1)} %compare_and_fusion.5), kind=kLoop, calls=%fused_computation.57.clone.1 | loop fusion | flops 4192256 | bytes 4276224 | tf_op jit(solution)/shard_map/while/body/eval_jaxpr/reduce_sum | solution.py:40
  133.4 2.9 %fusion.98 = f32[128,2,8,128]{0,3,2,1:T(8,128)S(1)} fusion(bf16[512,2,128,1]{0,2,3,1:T(8,128)(2,1)S(1)} %bitcast.127, f32[2,512,128,8]{2,1,3,0:T(8,128)S(1)} %copy-done.1, s32[512]{0:T(512)S(1)} %iota_add_fusion.13, s32[128,2,8]{0,2,1:T(8,128)S(1)} %fusion.97, f32[128,2,8]{0,2,1:T(8,128)S(1)} %select_maximum_fusion.5, ...), kind=kOutput, calls=%fused_computation.60.clone.1 | convolution fusion | flops 287047680 | bytes 6645761 | tf_op jit(solution)/shard_map/while/body/eval_jaxpr/qkgn,nkd->qkgd/dot_general | solution.py:46
  140.5 3.2 %fusion.95 = f32[128,2,8]{0,2,1:T(8,128)S(1)} fusion(f32[2,512,128,8]{2,1,3,0:T(8,128)} %get-tuple-element.726, f32[128,2,8]{0,2,1:T(8,128)S(1)} %select_maximum_fusion.5, pred[128,512]{0,1:T(8,128)(4,1)S(1)} %compare_and_fusion.5), kind=kLoop, calls=%fused_computation.57.clone.1 | loop fusion | flops 4192256 | bytes 4276224 | tf_op jit(solution)/shard_map/while/body/eval_jaxpr/reduce_sum | solution.py:40
  143.9 2.9 %fusion.98 = f32[128,2,8,128]{0,3,2,1:T(8,128)S(1)} fusion(bf16[512,2,128,1]{0,2,3,1:T(8,128)(2,1)S(1)} %bitcast.127, f32[2,512,128,8]{2,1,3,0:T(8,128)S(1)} %copy-done.1, s32[512]{0:T(512)S(1)} %iota_add_fusion.13, s32[128,2,8]{0,2,1:T(8,128)S(1)} %fusion.97, f32[128,2,8]{0,2,1:T(8,128)S(1)} %select_maximum_fusion.5, ...), kind=kOutput, calls=%fused_computation.60.clone.1 | convolution fusion | flops 287047680 | bytes 6645761 | tf_op jit(solution)/shard_map/while/body/eval_jaxpr/qkgn,nkd->qkgd/dot_general | solution.py:46
  147.1 16.7 %convolution_convert_fusion = bf16[256,8192]{1,0:T(8,128)(2,1)} fusion(bf16[2048,8192]{1,0:T(8,128)(2,1)} %param.13, bf16[128,2048]{0,1:T(8,128)(2,1)S(1)} %bitcast.129, bf16[128,2048]{0,1:T(8,128)(2,1)S(1)} %bitcast.128), kind=kOutput, calls=%fused_computation.84 | convolution fusion | flops 8594128896 | bytes 38797312 | tf_op jit(solution)/shard_map/dot_general | solution.py:114
  163.8 77.5 %reduce-scatter.2.cloned.1.call-done = bf16[256,2048]{1,0:T(8,128)(2,1)} async-done(((bf16[256,8192]{1,0:T(8,128)(2,1)}), bf16[256,2048]{1,0:T(8,128)(2,1)}) %reduce-scatter.2.cloned.1.call-update) | async-done | bytes 1048592 | tf_op jit(solution)/shard_map/reduce_scatter | solution.py:115
  (140 shorter events, 39.6 us)
Async XLA Ops:
  6.5 6.9 %copy-start.5 = (s32[2048]{0:T(1024)S(1)}, s32[2048]{0:T(1024)}, u32[]{:S(2)}) copy-start(s32[2048]{0:T(1024)} %param.14) | copy-start | bytes 24580
  6.5 26.9 %all-gather.3.cloned.1.call-start = ((), (), s32[]{:S(2)}) async-start(), calls=%async_computation.1 | async-start | bytes 1179648 | tf_op jit(solution)/shard_map/all_gather | solution.py:97
  8.2 50.7 %all-gather.5.cloned.1.call-start = ((), (), s32[]{:S(2)}) async-start(), calls=%async_computation.2 | async-start | bytes 1179648 | tf_op jit(solution)/shard_map/all_gather | solution.py:98
  10.0 231.3 %reduce-scatter.2.cloned.1.call-start = ((), (), s32[]{:S(2)}) async-start(), calls=%async_computation.3 | async-start | bytes 5242880 | tf_op jit(solution)/shard_map/reduce_scatter | solution.py:115
  60.3 6.1 %copy-start.2 = (f32[128,2,8,128]{0,3,2,1:T(8,128)S(1)}, f32[128,2,8,128]{0,3,2,1:T(8,128)}, u32[]{:S(2)}) copy-start(f32[128,2,8,128]{0,3,2,1:T(8,128)} %get-tuple-element.797) | copy-start | bytes 3145732 | tf_op jit(solution)/shard_map/while
  63.1 3.4 %copy-start = (f32[2,512,128,8]{2,1,3,0:T(8,128)S(1)}, f32[2,512,128,8]{2,1,3,0:T(8,128)}, u32[]{:S(2)}) copy-start(f32[2,512,128,8]{2,1,3,0:T(8,128)} %get-tuple-element.708) | copy-start | bytes 12582916 | tf_op jit(solution)/shard_map/while
  69.4 1.0 copy-start.3
  71.7 6.1 %copy-start.2 = (f32[128,2,8,128]{0,3,2,1:T(8,128)S(1)}, f32[128,2,8,128]{0,3,2,1:T(8,128)}, u32[]{:S(2)}) copy-start(f32[128,2,8,128]{0,3,2,1:T(8,128)} %get-tuple-element.797) | copy-start | bytes 3145732 | tf_op jit(solution)/shard_map/while
  74.5 3.4 %copy-start = (f32[2,512,128,8]{2,1,3,0:T(8,128)S(1)}, f32[2,512,128,8]{2,1,3,0:T(8,128)}, u32[]{:S(2)}) copy-start(f32[2,512,128,8]{2,1,3,0:T(8,128)} %get-tuple-element.708) | copy-start | bytes 12582916 | tf_op jit(solution)/shard_map/while
  80.9 1.0 copy-start.3
  83.2 6.1 %copy-start.2 = (f32[128,2,8,128]{0,3,2,1:T(8,128)S(1)}, f32[128,2,8,128]{0,3,2,1:T(8,128)}, u32[]{:S(2)}) copy-start(f32[128,2,8,128]{0,3,2,1:T(8,128)} %get-tuple-element.797) | copy-start | bytes 3145732 | tf_op jit(solution)/shard_map/while
  86.0 3.4 %copy-start = (f32[2,512,128,8]{2,1,3,0:T(8,128)S(1)}, f32[2,512,128,8]{2,1,3,0:T(8,128)}, u32[]{:S(2)}) copy-start(f32[2,512,128,8]{2,1,3,0:T(8,128)} %get-tuple-element.708) | copy-start | bytes 12582916 | tf_op jit(solution)/shard_map/while
  92.3 1.0 copy-start.3
  94.7 6.1 %copy-start.2 = (f32[128,2,8,128]{0,3,2,1:T(8,128)S(1)}, f32[128,2,8,128]{0,3,2,1:T(8,128)}, u32[]{:S(2)}) copy-start(f32[128,2,8,128]{0,3,2,1:T(8,128)} %get-tuple-element.797) | copy-start | bytes 3145732 | tf_op jit(solution)/shard_map/while
  97.5 3.4 %copy-start = (f32[2,512,128,8]{2,1,3,0:T(8,128)S(1)}, f32[2,512,128,8]{2,1,3,0:T(8,128)}, u32[]{:S(2)}) copy-start(f32[2,512,128,8]{2,1,3,0:T(8,128)} %get-tuple-element.708) | copy-start | bytes 12582916 | tf_op jit(solution)/shard_map/while
  103.8 1.0 copy-start.3
  104.8 42.1 %copy-start.4 = (f32[128,2,8,128]{0,3,2,1:T(8,128)S(1)}, f32[128,2,8,128]{0,3,2,1:T(8,128)}, u32[]{:S(2)}) copy-start(f32[128,2,8,128]{0,3,2,1:T(8,128)} %get-tuple-element.375) | copy-start | bytes 3145732
  109.0 3.4 %copy-start.1 = (f32[2,512,128,8]{2,1,3,0:T(8,128)S(1)}, f32[2,512,128,8]{2,1,3,0:T(8,128)}, u32[]{:S(2)}) copy-start(f32[2,512,128,8]{2,1,3,0:T(8,128)} %get-tuple-element.726) | copy-start | bytes 12582916 | tf_op jit(solution)/shard_map/while
  119.5 3.4 %copy-start.1 = (f32[2,512,128,8]{2,1,3,0:T(8,128)S(1)}, f32[2,512,128,8]{2,1,3,0:T(8,128)}, u32[]{:S(2)}) copy-start(f32[2,512,128,8]{2,1,3,0:T(8,128)} %get-tuple-element.726) | copy-start | bytes 12582916 | tf_op jit(solution)/shard_map/while
  130.0 3.4 %copy-start.1 = (f32[2,512,128,8]{2,1,3,0:T(8,128)S(1)}, f32[2,512,128,8]{2,1,3,0:T(8,128)}, u32[]{:S(2)}) copy-start(f32[2,512,128,8]{2,1,3,0:T(8,128)} %get-tuple-element.726) | copy-start | bytes 12582916 | tf_op jit(solution)/shard_map/while
  140.5 3.4 %copy-start.1 = (f32[2,512,128,8]{2,1,3,0:T(8,128)S(1)}, f32[2,512,128,8]{2,1,3,0:T(8,128)}, u32[]{:S(2)}) copy-start(f32[2,512,128,8]{2,1,3,0:T(8,128)} %get-tuple-element.726) | copy-start | bytes 12582916 | tf_op jit(solution)/shard_map/while
Sparse Core Ops, SparseCore 0:
  9.2 24.1 all-gather.2
  35.3 23.5 all-gather.4
  164.0 77.2 reduce-scatter.1
where the time goes:
time: 250 us; the launch traced here: 248 us
  waiting for transfers between devices  123 us (49%)
  matrix products  61.9 us (25%)
  other arithmetic  28.4 us (11%)
  local copies, waits for them, and re-layouts  19.9 us (8%)
  between operations  14.1 us (6%)
    reduce_scatter x1, waiting for transfers between devices, body(): lax.psum_scatter(partial_value.astype(jnp.bfloat16), 'tp', scatter_dimens...  77.5 us
    reduce_sum x8, other arithmetic, attend_tile(): row_sum = row_sum * rescale + jnp.sum(weights, axis=-1)  25.6 us
    all_gather x1, waiting for transfers between devices, body(): lax.all_gather(value_proj, 'ctx', axis=0, tiled=True)  25.5 us
    dot_general x8, matrix products, attend_tile(): jnp.einsum('qkgn,nkd->qkgd', dropped, v_heads, preferred_element_type=jnp...  23 us
    dot_general x8, matrix products, attend_tile(): jnp.einsum('qkgd,nkd->qkgn', q_heads, k_heads, preferred_element_type=jnp...  22.3 us
    all_gather x1, waiting for transfers between devices, body(): lax.all_gather(key_proj, 'ctx', axis=0, tiled=True)  19.9 us
    dot_general x1, matrix products, body(): jnp.dot(attention, out_weight, preferred_element_type=jnp.float32)  16.7 us
    dynamic_slice x8, local copies, waits for them, and re-layouts, step_tile(): v_tile = lax.dynamic_slice_in_dim(v_rows, offset, tile_rows, 0)  8.62 us
  transfers between devices with their start and end apart: 3, of which 3 were waited for; matrix products, arithmetic and copies ran while one was open for 2% of the time, Pallas kernels for 0%

commit v1 on v0

v1 whole, which is shorter than its diff:
```python
import functools

import jax
import jax.numpy as jnp
from jax import lax
from jax.experimental import pallas as pl
from jax.experimental.pallas import tpu as pltpu
from jax.sharding import PartitionSpec as P

HEADS = 64
KVH = 8
HD = 128
PAIR = 2
EXP2_SCALE = HD ** (-0.5) * 1.4426950408889634


def half_mixing(value):
    value = value ^ lax.shift_right_logical(value, jnp.int32(16))
    value = value * 73244475
    value = value ^ lax.shift_right_logical(value, jnp.int32(16))
    return value * 73244475


def mixing(value):
    value = half_mixing(value)
    return value ^ lax.shift_right_logical(value, jnp.int32(16))


def attend_kernel(meta_ref, q_ref, kv_ref, start_ref, out_ref):
    rows = q_ref.shape[0]
    pair = q_ref.shape[1] // HD
    step = pl.program_id(0)
    first_tile, block, seed, head_base = meta_ref[0], meta_ref[1], meta_ref[2], meta_ref[3]
    group = (step * pair) // (HEADS // KVH)
    q_pos = block * rows + lax.broadcasted_iota(jnp.int32, (1, rows), 1)
    doc_start = start_ref[...]
    k_iota = lax.broadcasted_iota(jnp.int32, (rows, rows), 0)
    hashes = []
    for n in range(pair):
        head = jnp.full((1, rows), head_base + step * pair + n, jnp.int32)
        hashes.append(mixing(mixing(seed * 7919 + head) ^ (q_pos * 65537)))

    def tile(number, state, diagonal):
        base = number * rows
        k_tile = kv_ref[number, group, 0:rows, :]
        v_tile = jnp.concatenate(
            [kv_ref[number, group, rows + HD * m : rows + HD * (m + 1), :] for m in range(rows // HD)],
            axis=1,
        )
        allowed = k_iota >= doc_start - base
        if diagonal:
            allowed = allowed & (k_iota <= q_pos - base)
        result = []
        for n in range(pair):
            q_head = q_ref[:, n * HD : (n + 1) * HD]
            scores = lax.dot_general(
                k_tile, q_head, (((1,), (1,)), ((), ())), preferred_element_type=jnp.float32
            )
            scores = jnp.where(allowed, scores, jnp.float32(-1e30))
            tile_max = jnp.max(scores, axis=0, keepdims=True)
            peak = tile_max if diagonal else jnp.maximum(state[n][0], tile_max)
            weights = jnp.exp2((scores - peak) * EXP2_SCALE)
            total = jnp.sum(weights, axis=0, keepdims=True)
            mixed = mixing((hashes[n] + base) + k_iota)
            keeper = lax.shift_right_logical(mixed, jnp.int32(8)) >= 1677722
            dropped = jnp.where(keeper, weights, jnp.float32(0.0)).astype(jnp.bfloat16)
            value = jnp.dot(v_tile, dropped, preferred_element_type=jnp.float32)
            if not diagonal:
                rescale = jnp.exp2((state[n][0] - peak) * EXP2_SCALE)
                total = state[n][1] * rescale + total
                value = state[n][2] * rescale + value
            result.append((peak, total, value))
        return tuple(result)

    state = tile(block, None, True)
    state = lax.fori_loop(first_tile, block, lambda i, s: tile(i, s, False), state)
    for n in range(pair):
        _, total, value = state[n]
        value = value * (jnp.float32(1.0 / 0.9) / total)
        out_ref[:, n * HD : (n + 1) * HD] = value.T.astype(jnp.bfloat16)


def attend(queries, kv_all, doc_ids, drop_seed):
    rows, width = queries.shape
    local_heads = width // HD
    ctx_index = lax.axis_index("ctx").astype(jnp.int32)
    tp_index = lax.axis_index("tp").astype(jnp.int32)
    q_doc = lax.dynamic_slice_in_dim(doc_ids, ctx_index * rows, rows)
    doc_start = jnp.sum((doc_ids[:, None] < q_doc[None, :]).astype(jnp.int32), axis=0)
    meta = jnp.stack([doc_start[0] // rows, ctx_index, drop_seed[0], tp_index * local_heads])
    return pl.pallas_call(
        attend_kernel,
        grid_spec=pltpu.PrefetchScalarGridSpec(
            num_scalar_prefetch=1,
            grid=(local_heads // PAIR,),
            in_specs=[
                pl.BlockSpec((rows, PAIR * HD), lambda i, m: (0, i)),
                pl.BlockSpec(kv_all.shape, lambda i, m: (0, 0, 0, 0)),
                pl.BlockSpec((1, rows), lambda i, m: (0, 0)),
            ],
            out_specs=pl.BlockSpec((rows, PAIR * HD), lambda i, m: (0, i)),
        ),
        out_shape=jax.ShapeDtypeStruct(queries.shape, jnp.bfloat16),
        compiler_params=pltpu.CompilerParams(vmem_limit_bytes=48 * 1024 * 1024),
    )(meta, queries, kv_all, doc_start.reshape(1, rows))


def pack_kv(key_proj, value_proj):
    rows = key_proj.shape[0]
    local_kv = key_proj.shape[1] // HD
    keys = key_proj.reshape(rows, local_kv, HD).transpose(1, 0, 2)
    values = value_proj.reshape(rows // HD, HD, local_kv, HD).transpose(2, 0, 3, 1)
    return jnp.concatenate([keys, values.reshape(local_kv, rows, HD)], axis=1)


def body(queries, key_proj, value_proj, out_weight, doc_ids, drop_seed):
    kv_all = lax.all_gather(pack_kv(key_proj, value_proj), "ctx", axis=0)
    attention = attend(queries, kv_all, doc_ids, drop_seed)
    partial_value = jnp.dot(attention, out_weight, preferred_element_type=jnp.float32)
    return lax.psum_scatter(
        partial_value.astype(jnp.bfloat16), "tp", scatter_dimension=1, tiled=True
    )


def solution(mesh):
    in_specs = (P("ctx", "tp"), P("ctx", "tp"), P("ctx", "tp"), P("tp", None), P(), P())
    out_specs = P("ctx", "tp")
    return jax.shard_map(body, mesh=mesh, in_specs=in_specs, out_specs=out_specs, check_vma=False)
```

time: 250 us -> 177 us (0.71); the launches traced: 248 us -> 179 us
  matrix products: 61.9 us -> 16.4 us
  other arithmetic: 28.4 us -> 1.14 us
  Pallas kernels: 0 us -> 15.7 us
  local copies, waits for them, and re-layouts: 19.9 us -> 7.16 us
  between operations: 14.1 us -> 16.6 us
    dot_general x16 -> x0, matrix products: 45.2 us -> none  [the longest x8 23 us: attend_tile(): jnp.einsum('qkgn,nkd->qkgd', dropped, v_heads, preferred_element_type=jnp...]
    reduce_sum x8 -> x1, other arithmetic: 25.6 us -> 1.05 us  [attend(): jnp.sum((doc_ids[:, None] < q_doc[None, :]).astype(jnp.int32), axis=0)]
    all_gather x2 -> x1, waiting for transfers between devices: 45.4 us -> 23 us  [body(): kv_all = lax.all_gather(pack_kv(key_proj, value_proj), 'ctx', axis=0)]
    reduce_scatter x1, waiting for transfers between devices: 77.5 us -> 98.5 us  [body(): lax.psum_scatter(partial_value.astype(jnp.bfloat16), 'tp', scatter_dimens...]
    pallas_call x0 -> x1, Pallas kernels: none -> 15.7 us  [attend(): pl.pallas_call(attend_kernel, grid_spec=pltpu.PrefetchScalarGridSpec(num_...]
    dynamic_slice x16 -> x1, local copies, waits for them, and re-layouts: 9.23 us -> 0.76 us  [attend(): q_doc = lax.dynamic_slice_in_dim(doc_ids, ctx_index * rows, rows)]
    while x40 -> x0, local copies, waits for them, and re-layouts: 4.96 us -> none
  transfers between devices with their start and end apart: 3 -> 2, of which waited for: 3 -> 2; matrix products, arithmetic and copies ran while one was open for 2% -> 1% of each run, Pallas kernels for 0% -> 0%
where the time goes in v1:
time: 177 us; the launch traced here: 179 us
  waiting for transfers between devices  122 us (69%)
  between operations  16.6 us (9%)
  matrix products  16.4 us (9%)
  Pallas kernels  15.7 us (9%)
  local copies, waits for them, and re-layouts  7.16 us (4%)
    reduce_scatter x1, waiting for transfers between devices, body(): lax.psum_scatter(partial_value.astype(jnp.bfloat16), 'tp', scatter_dimens...  98.5 us
    all_gather x1, waiting for transfers between devices, body(): kv_all = lax.all_gather(pack_kv(key_proj, value_proj), 'ctx', axis=0)  23 us
    dot_general x1, matrix products, body(): jnp.dot(attention, out_weight, preferred_element_type=jnp.float32)  16.4 us
    pallas_call x1, Pallas kernels, attend(): pl.pallas_call(attend_kernel, grid_spec=pltpu.PrefetchScalarGridSpec(num_...  15.7 us
    unnamed x5, local copies, waits for them, and re-layouts  3.82 us
  transfers between devices with their start and end apart: 2, of which 2 were waited for; matrix products, arithmetic and copies ran while one was open for 1% of the time, Pallas kernels for 0%

profile of v1, /device:TPU:15, one launch (start us, length us, event | category | flops | bytes accessed | tf_op | source)
XLA Modules:
  0.0 178.6 jit_solution(9108062033986413365)
XLA Ops:
  6.5 0.0 all-gather.3.cloned.1.call-start
  6.5 1.0 copy.13
  7.5 0.9 reshape.15
  8.5 0.1 copy.17
  8.6 0.1 reshape.16
  8.8 0.8 copy.15
  9.6 0.0 all-gather.3.cloned.1.call-update
  9.6 0.0 reduce-scatter.2.cloned.1.call-start
  9.7 0.8 dynamic_slice.3
  10.4 1.0 convert_reduce_fusion
  11.5 0.6 slice.3
  15.2 0.1 pad_add_fusion.meta_ref
  15.3 23.0 %all-gather.3.cloned.1.call-done = bf16[16,512,128]{2,1,0:T(8,128)(2,1)} async-done(((bf16[2,512,128]{2,1,0:T(8,128)(2,1)}), bf16[16,512,128]{2,1,0:T(8,128)(2,1)}) %all-gather.3.cloned.1.call-update) | async-done | bytes 2097168 | tf_op jit(solution)/shard_map/all_gather | solution.py:117
  38.3 0.0 copy-start
  38.3 1.6 copy-done
  39.9 0.0 copy-start.1
  39.9 1.2 copy-done.1
  41.1 15.7 %shard_map.64 = bf16[256,2048]{1,0:T(8,128)(2,1)S(1)} custom-call(s32[4]{0:T(128)S(1)} %pad_add_fusion.meta_ref, bf16[256,2048]{1,0:T(8,128)(2,1)S(1)} %copy-done.1, bf16[8,2,512,128]{3,2,1,0:T(8,128)(2,1)S(1)} %bitcast.16, s32[1,256]{1,0:T(1,128)S(1)} %bitcast.17), custom_call_target="tpu_custom_call" | custom-call | tf_op jit(solution)/shard_map/pallas_call | solution.py:91
  56.8 16.4 %convolution_convert_fusion = bf16[256,8192]{1,0:T(8,128)(2,1)} fusion(bf16[256,2048]{1,0:T(8,128)(2,1)S(1)} %shard_map.64, bf16[2048,8192]{1,0:T(8,128)(2,1)} %param.9), kind=kOutput, calls=%fused_computation | convolution fusion | flops 8592031744 | bytes 38797312 | tf_op jit(solution)/shard_map/dot_general | solution.py:119
  73.3 0.0 reduce-scatter.2.cloned.1.call-update
  73.3 98.5 %reduce-scatter.2.cloned.1.call-done = bf16[256,2048]{1,0:T(8,128)(2,1)} async-done(((bf16[256,8192]{1,0:T(8,128)(2,1)}), bf16[256,2048]{1,0:T(8,128)(2,1)}) %reduce-scatter.2.cloned.1.call-update) | async-done | bytes 1048592 | tf_op jit(solution)/shard_map/reduce_scatter | solution.py:120
  (1 shorter events, 0.0 us)
Async XLA Ops:
  6.5 31.7 %all-gather.3.cloned.1.call-start = ((), (), s32[]{:S(2)}) async-start(), calls=%async_computation.2 | async-start | bytes 2359296 | tf_op jit(solution)/shard_map/all_gather | solution.py:117
  9.6 162.2 %reduce-scatter.2.cloned.1.call-start = ((), (), s32[]{:S(2)}) async-start(), calls=%async_computation.1 | async-start | bytes 5242880 | tf_op jit(solution)/shard_map/reduce_scatter | solution.py:120
  38.3 1.6 copy-start
  39.9 1.2 copy-start.1
Sparse Core Ops, SparseCore 0:
  9.7 28.4 all-gather.2
  73.4 98.3 reduce-scatter.1

commit v2 on v1

--- a/solution.py
+++ b/solution.py
@@ -113,16 +113,182 @@
     return jnp.concatenate([keys, values.reshape(local_kv, rows, HD)], axis=1)
 
 
-def body(queries, key_proj, value_proj, out_weight, doc_ids, drop_seed):
+def project_kernel(size, subs, att_ref, weight_ref, out_ref, own, from_left, from_right, w_buf, w_sem, send_r, recv_r, send_l, recv_l):
+    me = lax.axis_index("tp")
+    width = w_buf.shape[2]
+    tiles = size * subs
+    slots = w_buf.shape[0]
+    upper = (2 * me) // size
+
+    def target(i):
+        k = i // subs
+        a = (k // 2) * (1 - k % 2) + (size - 1 - k // 2) * (k % 2)
+        return a * upper + (size - 1 - a) * (1 - upper)
+
+    def weight_copy(i):
+        column = pl.multiple_of((target(i) * subs + i % subs) * width, width)
+        return pltpu.make_async_copy(
+            weight_ref.at[:, pl.ds(column, width)], w_buf.at[i % slots], w_sem.at[i % slots]
+        )
+
+    def right_copy(t, s):
+        return pltpu.make_async_remote_copy(
+            src_ref=own.at[t, s], dst_ref=from_left.at[t, s], send_sem=send_r.at[t, s],
+            recv_sem=recv_r.at[t, s], device_id={"tp": lax.rem(me + 1, size)},
+            device_id_type=pl.DeviceIdType.MESH,
+        )
+
+    def left_copy(t, s):
+        return pltpu.make_async_remote_copy(
+            src_ref=own.at[t, s], dst_ref=from_right.at[t, s], send_sem=send_l.at[t, s],
+            recv_sem=recv_l.at[t, s], device_id={"tp": lax.rem(me + size - 1, size)},
+            device_id_type=pl.DeviceIdType.MESH,
+        )
+
+    for i in range(slots - 1):
+        weight_copy(i).start()
+    barrier = pltpu.get_barrier_semaphore()
+
+    @pl.when(me > 0)
+    def _():
+        pl.semaphore_signal(barrier, inc=1, device_id={"tp": me - 1}, device_id_type=pl.DeviceIdType.MESH)
+
+    @pl.when(me < size - 1)
+    def _():
+        pl.semaphore_signal(barrier, inc=1, device_id={"tp": me + 1}, device_id_type=pl.DeviceIdType.MESH)
+
+    @pl.when((me > 0) & (me < size - 1))
+    def _():
+        pl.semaphore_wait(barrier, 2)
+
+    @pl.when((me == 0) | (me == size - 1))
+    def _():
+        pl.semaphore_wait(barrier, 1)
+
+    def make_tile(i, carry):
+        @pl.when(i + slots - 1 < tiles)
+        def _():
+            weight_copy(i + slots - 1).start()
+
+        weight_copy(i).wait()
+        t, s = target(i), i % subs
+        own[t, s] = jnp.dot(
+            att_ref[...], w_buf[i % slots], preferred_element_type=jnp.float32
+        ).astype(jnp.bfloat16)
+
+        @pl.when((me == 0) & (t > 0))
+        def _():
+            right_copy(t, s).start()
+
+        @pl.when((me == size - 1) & (t < size - 1))
+        def _():
+            left_copy(t, s).start()
+
+        return carry
+
+    lax.fori_loop(0, tiles, make_tile, 0)
+
+    def add(ref, t, s):
+        total = own[t, s].astype(jnp.float32) + ref[t, s].astype(jnp.float32)
+        own[t, s] = total.astype(jnp.bfloat16)
+
+    def hand_on(i, carry):
+        s = i % subs
+        right_t = size - 1 - i // subs
+        left_t = i // subs
+
+        @pl.when((me > 0) & (right_t > me))
+        def _():
+            right_copy(right_t, s).wait_recv()
+            add(from_left, right_t, s)
+            right_copy(right_t, s).start()
+
+        @pl.when((me < size - 1) & (left_t < me))
+        def _():
+            left_copy(left_t, s).wait_recv()
+            add(from_right, left_t, s)
+            left_copy(left_t, s).start()
+
+        return carry
+
+    lax.fori_loop(0, tiles, hand_on, 0)
+
+    for s in range(subs):
+        columns = slice(s * width, (s + 1) * width)
+
+        @pl.when(me == 0)
+        def _():
+            left_copy(me, s).wait_recv()
+            out_ref[:, columns] = (
+                own[me, s].astype(jnp.float32) + from_right[me, s].astype(jnp.float32)
+            ).astype(jnp.bfloat16)
+
+        @pl.when(me == size - 1)
+        def _():
+            right_copy(me, s).wait_recv()
+            out_ref[:, columns] = (
+                own[me, s].astype(jnp.float32) + from_left[me, s].astype(jnp.float32)
+            ).astype(jnp.bfloat16)
+
+        @pl.when((me > 0) & (me < size - 1))
+        def _():
+            right_copy(me, s).wait_recv()
+            left_copy(me, s).wait_recv()
+            out_ref[:, columns] = (
+                own[me, s].astype(jnp.float32)
+                + from_left[me, s].astype(jnp.float32)
+                + from_right[me, s].astype(jnp.float32)
+            ).astype(jnp.bfloat16)
+
+    def drain(i, carry):
+        t, s = i // subs, i % subs
+
+        @pl.when(t > me)
+        def _():
+            right_copy(t, s).wait_send()
+
+        @pl.when(t < me)
+        def _():
+            left_copy(t, s).wait_send()
+
+        return carry
+
+    lax.fori_loop(0, tiles, drain, 0)
+
+
+def project(attention, out_weight, size):
+    rows, features = attention.shape
+    columns = out_weight.shape[1] // size
+    width = min(512, columns)
+    subs = columns // width
+    block = pltpu.VMEM((size, subs, rows, width), jnp.bfloat16)
+    sems = pltpu.SemaphoreType.DMA((size, subs))
+    return pl.pallas_call(
+        functools.partial(project_kernel, size, subs),
+        out_shape=jax.ShapeDtypeStruct((rows, columns), jnp.bfloat16),
+        in_specs=[pl.BlockSpec(memory_space=pltpu.VMEM), pl.BlockSpec(memory_space=pl.ANY)],
+        out_specs=pl.BlockSpec(memory_space=pltpu.VMEM),
+        scratch_shapes=[
+            block, block, block,
+            pltpu.VMEM((3, features, width), jnp.bfloat16),
+            pltpu.SemaphoreType.DMA((3,)),
+            sems, sems, sems, sems,
+        ],
+        compiler_params=pltpu.CompilerParams(
+            collective_id=0, has_side_effects=True, vmem_limit_bytes=48 * 1024 * 1024
+        ),
+    )(attention, out_weight)
+
+
+def body(size, queries, key_proj, value_proj, out_weight, doc_ids, drop_seed):
     kv_all = lax.all_gather(pack_kv(key_proj, value_proj), "ctx", axis=0)
     attention = attend(queries, kv_all, doc_ids, drop_seed)
-    partial_value = jnp.dot(attention, out_weight, preferred_element_type=jnp.float32)
-    return lax.psum_scatter(
-        partial_value.astype(jnp.bfloat16), "tp", scatter_dimension=1, tiled=True
-    )
+    return project(attention, out_weight, size)
 
 
 def solution(mesh):
     in_specs = (P("ctx", "tp"), P("ctx", "tp"), P("ctx", "tp"), P("tp", None), P(), P())
     out_specs = P("ctx", "tp")
-    return jax.shard_map(body, mesh=mesh, in_specs=in_specs, out_specs=out_specs, check_vma=False)
+    return jax.shard_map(
+        functools.partial(body, mesh.shape["tp"]), mesh=mesh, in_specs=in_specs, out_specs=out_specs, check_vma=False
+    )

time: 177 us -> 155 us (0.88)
  waiting for transfers between devices: 122 us -> 24.4 us
  Pallas kernels: 15.7 us -> 107 us
  matrix products: 16.4 us -> 0 us
    reduce_scatter x1 -> x0, waiting for transfers between devices: 98.5 us -> none  [body(): lax.psum_scatter(partial_value.astype(jnp.bfloat16), 'tp', scatter_dimens...]
    pallas_call x0 -> x1, Pallas kernels: none -> 77.3 us  [project(): pl.pallas_call(functools.partial(project_kernel, size, subs), out_shape=j...]
    dot_general x1 -> x0, matrix products: 16.4 us -> none  [body(): jnp.dot(attention, out_weight, preferred_element_type=jnp.float32)]
    pallas_call x1, Pallas kernels: 15.7 us -> 29.9 us  [attend(): pl.pallas_call(attend_kernel, grid_spec=pltpu.PrefetchScalarGridSpec(num_...]
    unnamed x5 -> x8, local copies, waits for them, and re-layouts: 3.82 us -> 3.66 us
  transfers between devices with their start and end apart: 2 -> 1, of which waited for: 2 -> 1; matrix products, arithmetic and copies ran while one was open for 1% -> 1% of each run, Pallas kernels for 0% -> 0%
where the time goes in v2:
time: 155 us
  Pallas kernels  107 us (69%)
  waiting for transfers between devices  24.4 us (16%)
  between operations  16.6 us (11%)
  local copies, waits for them, and re-layouts  6.28 us (4%)
    pallas_call x1, Pallas kernels, project(): pl.pallas_call(functools.partial(project_kernel, size, subs), out_shape=j...  77.3 us
    pallas_call x1, Pallas kernels, attend(): pl.pallas_call(attend_kernel, grid_spec=pltpu.PrefetchScalarGridSpec(num_...  29.9 us
    all_gather x1, waiting for transfers between devices, body(): kv_all = lax.all_gather(pack_kv(key_proj, value_proj), 'ctx', axis=0)  24.4 us
    unnamed x8, local copies, waits for them, and re-layouts  3.66 us
  transfers between devices with their start and end apart: 1, of which 1 were waited for; matrix products, arithmetic and copies ran while one was open for 1% of the time, Pallas kernels for 0%

profile of v2, /device:TPU:15, one launch (start us, length us, event | category | flops | bytes accessed | tf_op | source)
XLA Modules:
  0.0 155.0 jit_solution(6903496825329047386)
XLA Ops:
  6.5 0.0 copy-start.2
  6.5 0.0 copy-start.1
  6.5 0.0 all-gather.3.cloned.1.call-start
  6.5 1.1 copy.13
  7.6 0.9 reshape.15
  8.6 0.1 copy.17
  8.7 0.1 reshape.16
  8.9 0.8 copy.15
  9.7 0.0 all-gather.3.cloned.1.call-update
  9.7 0.0 copy-done.2
  9.7 0.1 dynamic_slice.3
  9.8 0.4 convert_reduce_fusion
  10.2 0.5 slice.3
  13.9 0.1 pad_add_fusion.meta_ref
  13.9 24.4 %all-gather.3.cloned.1.call-done = bf16[16,512,128]{2,1,0:T(8,128)(2,1)} async-done(((bf16[2,512,128]{2,1,0:T(8,128)(2,1)}), bf16[16,512,128]{2,1,0:T(8,128)(2,1)}) %all-gather.3.cloned.1.call-update) | async-done | bytes 2097168 | tf_op jit(solution)/shard_map/all_gather | solution.py:284
  38.4 0.0 copy-done.1
  38.4 0.0 copy-start
  38.4 1.6 %copy-done = bf16[16,512,128]{2,1,0:T(8,128)(2,1)S(1)} copy-done((bf16[16,512,128]{2,1,0:T(8,128)(2,1)S(1)}, bf16[16,512,128]{2,1,0:T(8,128)(2,1)}, u32[]{:S(2)}) %copy-start) | copy-done | bytes 2097176
  40.0 29.9 %shard_map.64.att_ref = bf16[256,2048]{1,0:T(8,128)(2,1)S(1)} custom-call(s32[4]{0:T(128)S(1)} %pad_add_fusion.meta_ref, bf16[256,2048]{1,0:T(8,128)(2,1)S(1)} %copy-done.1, bf16[8,2,512,128]{3,2,1,0:T(8,128)(2,1)S(1)} %bitcast.14, s32[1,256]{1,0:T(1,128)S(1)} %bitcast.15), custom_call_target="tpu_custom_call" | custom-call | tf_op jit(solution)/shard_map/pallas_call | solution.py:91
  69.8 77.3 %shard_map.65 = bf16[256,2048]{1,0:T(8,128)(2,1)S(1)} custom-call(bf16[256,2048]{1,0:T(8,128)(2,1)S(1)} %shard_map.64.att_ref, bf16[2048,8192]{1,0:T(8,128)(2,1)} %weight_ref.1), custom_call_target="tpu_custom_call" | custom-call | tf_op jit(solution)/shard_map/pallas_call | solution.py:266
  147.2 1.0 copy.20
  (1 shorter events, 0.0 us)
Async XLA Ops:
  6.5 3.2 %copy-start.2 = (s32[2048]{0:T(1024)S(1)}, s32[2048]{0:T(1024)}, u32[]{:S(2)}) copy-start(s32[2048]{0:T(1024)} %param.10) | copy-start | bytes 24580
  6.5 31.8 %copy-start.1 = (bf16[256,2048]{1,0:T(8,128)(2,1)S(1)}, bf16[256,2048]{1,0:T(8,128)(2,1)}, u32[]{:S(2)}) copy-start(bf16[256,2048]{1,0:T(8,128)(2,1)} %q_ref.1) | copy-start | bytes 3145732
  6.5 31.8 %all-gather.3.cloned.1.call-start = ((), (), s32[]{:S(2)}) async-start(), calls=%async_computation | async-start | bytes 2359296 | tf_op jit(solution)/shard_map/all_gather | solution.py:284
  38.4 1.6 %copy-start = (bf16[16,512,128]{2,1,0:T(8,128)(2,1)S(1)}, bf16[16,512,128]{2,1,0:T(8,128)(2,1)}, u32[]{:S(2)}) copy-start(bf16[16,512,128]{2,1,0:T(8,128)(2,1)} %all-gather.3.cloned.1.call-done) | copy-start | bytes 6291460
Sparse Core Ops, SparseCore 0:
  9.8 28.4 all-gather.2
